TPU v7x, 32 devices: a whole 2x2x4 slice. The times are simulated.
32 devices in a mesh: slides: 2 (over y), tile: 4 (over z), col: 2 (over x), mp: 2 (over core).
Axes of the slice: x: 2, y: 2, z: 4, core: 2. Of those that a mesh axis runs over, the one named last changes fastest.
Arguments:
- patches: bfloat16 [128, 48, 1024], P(('slides', 'tile'), 'col', 'mp'), parts along dimension 0, may hold values from -8 to 8
- tissue: int32 [128, 48], P(('slides', 'tile'), 'col'), parts along dimension 0, may hold values from 0 to 1, as said below
- conv_weight: bfloat16 [3, 3, 1024], P(None, None, 'mp'), may hold values from -2 to 2
- ln_gain: float32 [1024], P('mp'), may hold values from 0.1 to 1.9
- qkv_weight: bfloat16 [3, 1024, 1024], P(None, None, 'mp'), may hold values from -0.1875 to 0.1875
- omega: float32 [256, 64], replicated, may hold values from -6 to 6
- out_weight: bfloat16 [1024, 1024], P('mp'), may hold values from -0.1875 to 0.1875
Outputs:
- layer_out: bfloat16 [128, 48, 1024], P(('slides', 'tile'), 'col', 'mp'), parts along dimension 0
There are 2 independent parts, one for each index of `slides`. A program takes and returns all parts, laid end to end along the dimension named above; an argument that names none is the same for every part. Nothing has to cross between parts.
Inputs may be any that keep to these rules, and one draw needn't show every extreme that they name: 1 marks tissue, 0 background; the slide's first patch is tissue.
All inputs are finite; a program needn't handle non-finite values.
Results may differ from a plain program's by a relative error of at most 0.0065.
Values may be sent and summed in bfloat16 or wider, within the bound.
A program may use at most 64 MiB of HBM per device.

v0:
```python
import math
import jax
import jax.numpy as jnp
from jax import lax
from jax.sharding import PartitionSpec as P

E = 64
M = 256


def extended(cells, sides, width):
    for axis, dim in sides:
        count = lax.axis_size(axis)
        ends = count - 1
        head = lax.slice_in_dim(cells, 0, width, axis=dim)
        tail = lax.slice_in_dim(cells, cells.shape[dim] - width, cells.shape[dim], axis=dim)
        cells = jnp.concatenate(
            [
                lax.ppermute(tail, axis, [(i, (i + 1) % count) for i in range(ends)]),
                cells,
                lax.ppermute(head, axis, [((i + 1) % count, i) for i in range(ends)]),
            ],
            axis=dim,
        )
    return cells


def features(scaled, omega):
    lifted = jnp.einsum("the,me->thm", scaled, omega, precision=lax.Precision.HIGHEST)
    square = 0.5 * jnp.sum(scaled * scaled, axis=-1, keepdims=True)
    return (jnp.exp(lifted - square) / math.sqrt(M)).astype(jnp.bfloat16)


def split_pair(values):
    upper = values.astype(jnp.bfloat16)
    lower = (values - upper.astype(jnp.float32)).astype(jnp.bfloat16)
    return (upper, lower)


def shards(patches, tissue, conv_weight, ln_gain, qkv_weight, omega, out_weight):
    rows_here, cols_here, half = patches.shape
    tokens = rows_here * cols_here
    padded = extended(patches, (("tile", 0), ("col", 1)), 1)
    widened = padded.astype(jnp.float32)
    kernel = conv_weight.astype(jnp.float32)
    stem = patches.astype(jnp.float32)
    for row_off in range(3):
        for col_off in range(3):
            stem = (
                stem
                + kernel[row_off, col_off]
                * widened[row_off : row_off + rows_here, col_off : col_off + cols_here]
            )
    flat = stem.reshape(tokens, half)
    totals = lax.psum((jnp.sum(flat, axis=1), jnp.sum(flat * flat, axis=1)), "mp")
    width = half * lax.axis_size("mp")
    mean_val = totals[0] / width
    var_val = totals[1] / width - mean_val * mean_val
    normed = ((flat - mean_val[:, None]) * lax.rsqrt(var_val + 1e-05)[:, None] * ln_gain).astype(
        jnp.bfloat16
    )
    projected = jnp.einsum(
        "td,cdf->ctf",
        lax.all_gather(normed, "mp", axis=1, tiled=True),
        qkv_weight,
        preferred_element_type=jnp.float32,
    ).astype(jnp.bfloat16)
    heads_here = qkv_weight.shape[2] // E
    scale = E ** (-0.25)
    key_part = projected[1].astype(jnp.float32).reshape(tokens, heads_here, E) * scale
    keep = tissue.reshape(tokens).astype(jnp.bfloat16)
    key_feat = features(key_part, omega) * keep[:, None, None]
    value_part = projected[2].reshape(tokens, heads_here, E)
    state = jnp.einsum("the,thm->hem", value_part, key_feat, preferred_element_type=jnp.float32)
    key_sum = jnp.sum(key_feat.astype(jnp.float32), axis=0)
    kv_state, normalizer = lax.psum((state, key_sum), ("tile", "col"))
    query_part = projected[0].astype(jnp.float32).reshape(tokens, heads_here, E) * scale
    query_feat = features(query_part, omega)
    state_upper, state_lower = split_pair(kv_state)
    norm_upper, norm_lower = split_pair(normalizer)
    numer = jnp.einsum("thm,hem->the", query_feat, state_upper, preferred_element_type=jnp.float32)
    numer = numer + jnp.einsum(
        "thm,hem->the", query_feat, state_lower, preferred_element_type=jnp.float32
    )
    denom = jnp.einsum("thm,hm->th", query_feat, norm_upper, preferred_element_type=jnp.float32)
    denom = denom + jnp.einsum(
        "thm,hm->th", query_feat, norm_lower, preferred_element_type=jnp.float32
    )
    attended = (numer / denom[:, :, None]).astype(jnp.bfloat16).reshape(tokens, heads_here * E)
    mixed = (
        lax.psum_scatter(
            lax.dot_general(
                out_weight, attended, (((0,), (1,)), ((), ())), preferred_element_type=jnp.float32
            ).astype(jnp.bfloat16),
            "mp",
            scatter_dimension=0,
            tiled=True,
        )
        .astype(jnp.float32)
        .T
    )
    return (flat + mixed).astype(jnp.bfloat16).reshape(rows_here, cols_here, half)


def solution(mesh):
    placed = (
        P(("slides", "tile"), "col", "mp"),
        P(("slides", "tile"), "col"),
        P(None, None, "mp"),
        P("mp"),
        P(None, None, "mp"),
        P(),
        P("mp", None),
    )
    return jax.shard_map(
        shards,
        mesh=mesh,
        in_specs=placed,
        out_specs=P(("slides", "tile"), "col", "mp"),
        check_vma=False,
    )
```

profile of v0, /device:TPU:0, one launch (start us, length us, event | category | flops | bytes accessed | tf_op | source)
XLA Modules:
  0.0 167.3 jit_solution(4556089762340972274)
XLA Ops:
  7.5 5.0 %collective-permute-start = (bf16[1,24,512]{2,1,0:T(8,128)(2,1)S(1)}, bf16[1,24,512]{2,1,0:T(8,128)(2,1)S(1)}, u32[]{:S(2)}, u32[]{:S(2)}) collective-permute-start(bf16[1,24,512]{2,1,0:T(8,128)(2,1)S(1)} %get-tuple-element.15), channel_id=1, source_target_pairs={{0,4},{4,8},{8,12},{1,5},{5,9},{9,13},{2,6},{6,10},{10,14},{3,7},{... | collective-permute-start | bytes 73736 | tf_op jit(solution)/shard_map/ppermute | solution.py:19
  12.5 1.3 collective-permute-start.1
  15.0 3.2 %collective-permute-done.1 = bf16[1,24,512]{2,1,0:T(8,128)(2,1)S(1)} collective-permute-done((bf16[1,24,512]{2,1,0:T(8,128)(2,1)S(1)}, bf16[1,24,512]{2,1,0:T(8,128)(2,1)S(1)}, u32[]{:S(2)}, u32[]{:S(2)}) %collective-permute-start.1) | collective-permute-done | bytes 24608 | tf_op jit(solution)/shard_map/ppermute | solution.py:21
  19.7 4.0 %collective-permute-start.2 = (bf16[18,1,512]{2,1,0:T(2,128)(2,1)}, bf16[18,1,512]{2,1,0:T(2,128)(2,1)}, u32[]{:S(2)}, u32[]{:S(2)}) collective-permute-start(bf16[18,1,512]{2,1,0:T(2,128)(2,1)} %get-tuple-element.12), channel_id=1, source_target_pairs={{0,2},{1,3},{4,6},{5,7},{8,10},{9,11},{12,14},{13,15},{16,18},{17,... | collective-permute-start | bytes 55304 | tf_op jit(solution)/shard_map/ppermute | solution.py:19
  23.7 1.3 collective-permute-start.3
  25.0 1.5 fusion.35
  27.9 2.0 %collective-permute-done.3 = bf16[18,1,512]{2,1,0:T(2,128)(2,1)} collective-permute-done((bf16[18,1,512]{2,1,0:T(2,128)(2,1)}, bf16[18,1,512]{2,1,0:T(2,128)(2,1)}, u32[]{:S(2)}, u32[]{:S(2)}) %collective-permute-start.3) | collective-permute-done | bytes 18464 | tf_op jit(solution)/shard_map/ppermute | solution.py:21
  31.2 1.7 %fusion.31 = (f32[16,24]{1,0:T(8,128)S(1)}, f32[16,24]{1,0:T(8,128)S(1)}, f32[16,24,512]{2,1,0:T(8,128)}) fusion(f32[18,26,512]{2,1,0:T(8,128)S(1)} %maximum_convert_fusion, f32[512]{0:T(512)S(1)} %bitcast.83, f32[512]{0:T(512)S(1)} %bitcast.82, f32[512]{0:T(512)S(1)} %bitcast.81, f32[512]{0:T(512)S(1)} %bitcast.80, f32[512]{0:T(512)S(1)} %bitcast.79, ...), kind=kLoop, calls=%fused_computation.65 | loop fusion | flops 4324608 | bytes 8279040 | tf_op jit(solution)/shard_map/reduce_sum | solution.py:55
  33.1 2.5 %all-reduce = (f32[384]{0:T(512)S(1)}, f32[384]{0:T(512)S(1)}) all-reduce(f32[384]{0:T(512)S(1)} %reduce_sum.52, f32[384]{0:T(512)S(1)} %reduce_sum.50), channel_id=1, replica_groups=mesh['slides'=2,'tile'=4,'col'=2,'mp'=2] {'mp'}, use_global_device_ids=true, to_apply=%region_3.0 | all-reduce | flops 768 | bytes 6144 | tf_op jit(solution)/shard_map/psum | solution.py:55
  35.6 1.3 fusion.19
  36.9 2.4 %all_gather.3 = bf16[384,1024]{1,0:T(8,128)(2,1)S(1)} all-gather(bf16[384,512]{1,0:T(8,128)(2,1)S(1)} %fusion.19), channel_id=1, replica_groups=mesh['slides'=2,'tile'=4,'col'=2,'mp'=2] {'mp'}, dimensions={1}, use_global_device_ids=true | all-gather | bytes 1179648 | tf_op jit(solution)/shard_map/all_gather | solution.py:64
  39.3 1.4 fusion.1
  41.4 1.4 convert_multiply_fusion.1
  44.0 2.3 %copy.12 = f32[1,384,512]{1,2,0:T(8,128)} copy(f32[1,384,512]{2,1,0:T(8,128)} %get-tuple-element.10) | data formatting | bytes 1572864 | tf_op jit(solution)/shard_map/mul | solution.py:70
  47.6 5.8 %convert_reduce_fusion = (f32[8,256]{1,0:T(8,128)S(1)}, bf16[384,8,256]{2,0,1:T(8,128)(2,1)}) fusion(bf16[384]{0:T(512)(128)(2,1)S(1)} %copy-done.15, f32[384,8]{0,1:T(8,128)S(1)} %broadcast_multiply_fusion.1, f32[384,8,64]{0,2,1:T(8,128)} %bitcast.71, f32[256,64]{0,1:T(8,128)} %param.12), kind=kOutput, calls=%fused_computation | convolution fusion | flops 608696320 | bytes 2446080 | tf_op jit(solution)/shard_map/the,me->thm/dot_general | solution.py:29
  53.3 19.8 %psum.31 = f32[8,256]{1,0:T(8,128)S(1)} all-reduce(f32[8,256]{1,0:T(8,128)S(1)} %get-tuple-element.29), channel_id=1, replica_groups=mesh['slides'=2,'tile'=4,'col'=2,'mp'=2] {'tile','col'}, use_global_device_ids=true, to_apply=%region_8.0 | all-reduce | flops 2048 | bytes 16384 | tf_op jit(solution)/shard_map/psum | solution.py:76
  73.1 2.6 %fusion.36 = f32[8,64,256]{2,1,0:T(8,128)} fusion(bf16[384,8,64]{0,2,1:T(8,128)(2,1)S(1)} %bitcast.74, bf16[384,8,256]{2,0,1:T(8,128)(2,1)} %get-tuple-element.30), kind=kOutput, calls=%fused_computation.69 | convolution fusion | flops 100663296 | bytes 2490368 | tf_op jit(solution)/shard_map/the,thm->hem/dot_general | solution.py:74
  76.0 2.3 %copy.13 = f32[1,384,512]{1,2,0:T(8,128)} copy(f32[1,384,512]{2,1,0:T(8,128)} %get-tuple-element.11) | data formatting | bytes 1572864 | tf_op jit(solution)/shard_map/mul | solution.py:77
  79.5 4.4 %multiply_convert_fusion = bf16[384,8,256]{2,0,1:T(8,128)(2,1)S(1)} fusion(f32[384,8,64]{0,2,1:T(8,128)} %bitcast.73, f32[384,8]{0,1:T(8,128)S(1)} %broadcast_multiply_fusion, f32[256,64]{0,1:T(8,128)S(1)} %copy-done.17), kind=kOutput, calls=%fused_computation.1 | convolution fusion | flops 606339072 | bytes 2437120 | tf_op jit(solution)/shard_map/the,me->thm/dot_general | solution.py:29
  85.0 60.6 %all-reduce.3.cloned.1.call-done = f32[8,64,256]{2,1,0:T(8,128)} async-done(((f32[8,64,256]{2,1,0:T(8,128)}), f32[8,64,256]{2,1,0:T(8,128)}) %all-reduce.3.cloned.1.call-update) | async-done | bytes 524304 | tf_op jit(solution)/shard_map/psum | solution.py:76
  145.6 2.3 %fusion.21 = f32[8,64,384]{2,1,0:T(8,128)S(1)} fusion(bf16[384,8,256]{2,0,1:T(8,128)(2,1)} %copy-done.1, f32[8,64,256]{2,1,0:T(8,128)} %all-reduce.3.cloned.1.call-done), kind=kOutput, calls=%fused_computation.45 | convolution fusion | flops 100794368 | bytes 2883584 | tf_op jit(solution)/shard_map/thm,hem->the/dot_general | solution.py:81
  149.2 1.5 fusion.2
  150.7 7.7 %reduce-scatter.2.cloned.1.call-done = bf16[512,384]{0,1:T(8,128)(2,1)} async-done(((bf16[1024,384]{0,1:T(8,128)(2,1)}), bf16[512,384]{0,1:T(8,128)(2,1)}) %reduce-scatter.2.cloned.1.call-update) | async-done | bytes 393232 | tf_op jit(solution)/shard_map/reduce_scatter | solution.py:91
  158.3 2.1 %fusion.15 = bf16[384,512]{1,0:T(8,128)(2,1)} fusion(f32[16,24,512]{2,1,0:T(8,128)} %get-tuple-element.9, bf16[512,384]{0,1:T(8,128)(2,1)} %reduce-scatter.2.cloned.1.call-done), kind=kLoop, calls=%fused_computation.31 | loop fusion | flops 589824 | bytes 1572864 | tf_op jit(solution)/shard_map/convert_element_type | solution.py:102
  (64 shorter events, 13.4 us)
Async XLA Ops:
  6.5 32.7 %copy-start = (bf16[3,1024,512]{2,1,0:T(8,128)(2,1)S(1)}, bf16[3,1024,512]{2,1,0:T(8,128)(2,1)}, u32[]{:S(2)}) copy-start(bf16[3,1024,512]{2,1,0:T(8,128)(2,1)} %param.11) | copy-start | bytes 9437188
  6.5 24.6 %copy-start.3 = (bf16[16,24,512]{2,1,0:T(8,128)(2,1)S(1)}, bf16[16,24,512]{2,1,0:T(8,128)(2,1)}, u32[]{:S(2)}) copy-start(bf16[16,24,512]{2,1,0:T(8,128)(2,1)} %param.7) | copy-start | bytes 1179652
  6.5 139.1 %all-reduce.3.cloned.1.call-start = ((), (), s32[]{:S(2)}) async-start(), calls=%async_computation.1 | async-start | bytes 1048576 | tf_op jit(solution)/shard_map/psum | solution.py:76
  7.5 6.6 %collective-permute-start = (bf16[1,24,512]{2,1,0:T(8,128)(2,1)S(1)}, bf16[1,24,512]{2,1,0:T(8,128)(2,1)S(1)}, u32[]{:S(2)}, u32[]{:S(2)}) collective-permute-start(bf16[1,24,512]{2,1,0:T(8,128)(2,1)S(1)} %get-tuple-element.15), channel_id=1, source_target_pairs={{0,4},{4,8},{8,12},{1,5},{5,9},{9,13},{2,6},{6,10},{10,14},{3,7},{... | collective-permute-start | bytes 73736 | tf_op jit(solution)/shard_map/ppermute | solution.py:19
  12.5 5.7 %collective-permute-start.1 = (bf16[1,24,512]{2,1,0:T(8,128)(2,1)S(1)}, bf16[1,24,512]{2,1,0:T(8,128)(2,1)S(1)}, u32[]{:S(2)}, u32[]{:S(2)}) collective-permute-start(bf16[1,24,512]{2,1,0:T(8,128)(2,1)S(1)} %get-tuple-element.14), channel_id=1, source_target_pairs={{4,0},{8,4},{12,8},{5,1},{9,5},{13,9},{6,2},{10,6},{14,10},{7,3},{... | collective-permute-start | bytes 73736 | tf_op jit(solution)/shard_map/ppermute | solution.py:21
  18.2 0.8 copy-start.4
  19.7 8.2 %collective-permute-start.2 = (bf16[18,1,512]{2,1,0:T(2,128)(2,1)}, bf16[18,1,512]{2,1,0:T(2,128)(2,1)}, u32[]{:S(2)}, u32[]{:S(2)}) collective-permute-start(bf16[18,1,512]{2,1,0:T(2,128)(2,1)} %get-tuple-element.12), channel_id=1, source_target_pairs={{0,2},{1,3},{4,6},{5,7},{8,10},{9,11},{12,14},{13,15},{16,18},{17,... | collective-permute-start | bytes 55304 | tf_op jit(solution)/shard_map/ppermute | solution.py:19
  23.7 6.2 %collective-permute-start.3 = (bf16[18,1,512]{2,1,0:T(2,128)(2,1)}, bf16[18,1,512]{2,1,0:T(2,128)(2,1)}, u32[]{:S(2)}, u32[]{:S(2)}) collective-permute-start(bf16[18,1,512]{2,1,0:T(2,128)(2,1)} %get-tuple-element.13), channel_id=1, source_target_pairs={{2,0},{3,1},{6,4},{7,5},{10,8},{11,9},{14,12},{15,13},{18,16},{19,... | collective-permute-start | bytes 55304 | tf_op jit(solution)/shard_map/ppermute | solution.py:21
  27.8 3.3 %copy-start.6 = (f32[1,1,512]{2,1,0:T(1,128)S(1)}, f32[1,1,512]{2,1,0:T(1,128)}, u32[]{:S(2)}) copy-start(f32[1,1,512]{2,1,0:T(1,128)} %get-tuple-element.16) | copy-start | bytes 6148
  27.8 3.3 %copy-start.7 = (f32[1,1,512]{2,1,0:T(1,128)S(1)}, f32[1,1,512]{2,1,0:T(1,128)}, u32[]{:S(2)}) copy-start(f32[1,1,512]{2,1,0:T(1,128)} %get-tuple-element.17) | copy-start | bytes 6148
  27.8 3.3 %copy-start.8 = (f32[1,1,512]{2,1,0:T(1,128)S(1)}, f32[1,1,512]{2,1,0:T(1,128)}, u32[]{:S(2)}) copy-start(f32[1,1,512]{2,1,0:T(1,128)} %get-tuple-element.18) | copy-start | bytes 6148
  27.8 3.3 %copy-start.9 = (f32[1,1,512]{2,1,0:T(1,128)S(1)}, f32[1,1,512]{2,1,0:T(1,128)}, u32[]{:S(2)}) copy-start(f32[1,1,512]{2,1,0:T(1,128)} %get-tuple-element.19) | copy-start | bytes 6148
  27.8 3.4 %copy-start.10 = (f32[1,1,512]{2,1,0:T(1,128)S(1)}, f32[1,1,512]{2,1,0:T(1,128)}, u32[]{:S(2)}) copy-start(f32[1,1,512]{2,1,0:T(1,128)} %get-tuple-element.20) | copy-start | bytes 6148
  27.8 3.4 %copy-start.11 = (f32[1,1,512]{2,1,0:T(1,128)S(1)}, f32[1,1,512]{2,1,0:T(1,128)}, u32[]{:S(2)}) copy-start(f32[1,1,512]{2,1,0:T(1,128)} %get-tuple-element.21) | copy-start | bytes 6148
  27.8 3.4 %copy-start.12 = (f32[1,1,512]{2,1,0:T(1,128)S(1)}, f32[1,1,512]{2,1,0:T(1,128)}, u32[]{:S(2)}) copy-start(f32[1,1,512]{2,1,0:T(1,128)} %get-tuple-element.22) | copy-start | bytes 6148
  27.8 3.4 %copy-start.13 = (f32[1,1,512]{2,1,0:T(1,128)S(1)}, f32[1,1,512]{2,1,0:T(1,128)}, u32[]{:S(2)}) copy-start(f32[1,1,512]{2,1,0:T(1,128)} %get-tuple-element.23) | copy-start | bytes 6148
  27.8 3.4 %copy-start.14 = (f32[1,1,512]{2,1,0:T(1,128)S(1)}, f32[1,1,512]{2,1,0:T(1,128)}, u32[]{:S(2)}) copy-start(f32[1,1,512]{2,1,0:T(1,128)} %get-tuple-element.24) | copy-start | bytes 6148
  42.8 4.7 %copy-start.15 = (bf16[384]{0:T(512)(128)(2,1)S(1)}, bf16[384]{0:T(512)(128)(2,1)}, u32[]{:S(2)}) copy-start(bf16[384]{0:T(512)(128)(2,1)} %convert_element_type.95) | copy-start | bytes 2308
  75.7 3.8 %copy-start.17 = (f32[256,64]{0,1:T(8,128)S(1)}, f32[256,64]{0,1:T(8,128)}, u32[]{:S(2)}) copy-start(f32[256,64]{0,1:T(8,128)} %param.12) | copy-start | bytes 196612
  75.7 82.6 %reduce-scatter.2.cloned.1.call-start = ((), (), s32[]{:S(2)}) async-start(), calls=%async_computation.2 | async-start | bytes 1179648 | tf_op jit(solution)/shard_map/reduce_scatter | solution.py:91
  83.9 1.2 copy-start.1
  145.6 2.3 %copy-start.2 = (bf16[384,8,256]{2,0,1:T(8,128)(2,1)S(1)}, bf16[384,8,256]{2,0,1:T(8,128)(2,1)}, u32[]{:S(2)}) copy-start(bf16[384,8,256]{2,0,1:T(8,128)(2,1)} %copy-done.1) | copy-start | bytes 4718596
  145.6 2.3 %copy-start.5 = (f32[8,64,256]{2,1,0:T(8,128)S(1)}, f32[8,64,256]{2,1,0:T(8,128)}, u32[]{:S(2)}) copy-start(f32[8,64,256]{2,1,0:T(8,128)} %all-reduce.3.cloned.1.call-done) | copy-start | bytes 1572868
  147.9 1.2 copy-start.16
Sparse Core Ops, SparseCore 0:
  75.9 69.6 all-reduce.2
  150.8 7.5 reduce-scatter.1
where the time goes:
time: 168 us; the launch traced here: 167 us
  waiting for transfers between devices  73.7 us (44%)
  blocking collectives  24.6 us (15%)
  matrix products  19.5 us (12%)
  between operations  13.7 us (8%)
  local copies, waits for them, and re-layouts  13 us (8%)
  starting transfers between devices  11.8 us (7%)
  other arithmetic  10.9 us (6%)
    psum x1, waiting for transfers between devices, shards(): kv_state, normalizer = lax.psum((state, key_sum), ('tile', 'col'))  60.6 us
    psum x1, blocking collectives, shards(): kv_state, normalizer = lax.psum((state, key_sum), ('tile', 'col'))  19.8 us
    dot_general x2, matrix products, features(): jnp.einsum('the,me->thm', scaled, omega, precision=lax.Precision.HIGHEST)  10.1 us
    ppermute x2, starting transfers between devices, extended(): lax.ppermute(tail, axis, [(i, (i + 1) % count) for i in range(ends)])  9.05 us
    reduce_scatter x1, waiting for transfers between devices, shards(): lax.psum_scatter(lax.dot_general(out_weight, attended, (((0,), (1,)), (()...  7.69 us
    ppermute x2, waiting for transfers between devices, extended(): lax.ppermute(head, axis, [((i + 1) % count, i) for i in range(ends)])  5.17 us
  transfers between devices with their start and end apart: 6, of which 5 were waited for; matrix products, arithmetic and copies ran while one was open for 8% of the time, Pallas kernels for 0%

commit v1 on v0

--- a/solution.py
+++ b/solution.py
@@ -6,6 +6,11 @@
 
 E = 64
 M = 256
+
+
+def axis_by_axis(value, inner_axis, outer_axis):
+    inner = lax.psum(value, inner_axis)
+    return lax.psum(inner, outer_axis)
 
 
 def extended(cells, sides, width):
@@ -73,7 +78,7 @@
     value_part = projected[2].reshape(tokens, heads_here, E)
     state = jnp.einsum("the,thm->hem", value_part, key_feat, preferred_element_type=jnp.float32)
     key_sum = jnp.sum(key_feat.astype(jnp.float32), axis=0)
-    kv_state, normalizer = lax.psum((state, key_sum), ("tile", "col"))
+    kv_state, normalizer = axis_by_axis((state, key_sum), "col", "tile")
     query_part = projected[0].astype(jnp.float32).reshape(tokens, heads_here, E) * scale
     query_feat = features(query_part, omega)
     state_upper, state_lower = split_pair(kv_state)

time: 168 us -> 162 us (0.964)
  blocking collectives: 24.6 us -> 20.1 us
  waiting for transfers between devices: 73.7 us -> 69.7 us
  matrix products: 19.5 us -> 22.2 us
    psum x1 -> x2, waiting for transfers between devices: 60.6 us -> 55.8 us  [the longest x1 38.2 us: axis_by_axis(): return lax.psum(inner, outer_axis)]
    psum x1 -> x2, blocking collectives: 19.8 us -> 15.2 us  [the longest x1 10.3 us: axis_by_axis(): return lax.psum(inner, outer_axis)]
  transfers between devices with their start and end apart: 6 -> 7, of which waited for: 5 -> 6; matrix products, arithmetic and copies ran while one was open for 8% -> 10% of each run, Pallas kernels for 0% -> 0%
where the time goes in v1:
time: 162 us; the launch traced here: 161 us
  waiting for transfers between devices  69.7 us (43%)
  matrix products  22.2 us (14%)
  blocking collectives  20.1 us (12%)
  between operations  13.4 us (8%)
  local copies, waits for them, and re-layouts  12.9 us (8%)
  starting transfers between devices  11.7 us (7%)
  other arithmetic  10.9 us (7%)
    psum x1, waiting for transfers between devices, axis_by_axis(): return lax.psum(inner, outer_axis)  38.2 us
    psum x1, waiting for transfers between devices, axis_by_axis(): inner = lax.psum(value, inner_axis)  17.7 us
    dot_general x2, matrix products, features(): jnp.einsum('the,me->thm', scaled, omega, precision=lax.Precision.HIGHEST)  11.3 us
    psum x1, blocking collectives, axis_by_axis(): return lax.psum(inner, outer_axis)  10.3 us
    ppermute x2, starting transfers between devices, extended(): lax.ppermute(tail, axis, [(i, (i + 1) % count) for i in range(ends)])  9.04 us
    reduce_scatter x1, waiting for transfers between devices, shards(): lax.psum_scatter(lax.dot_general(out_weight, attended, (((0,), (1,)), (()...  8.39 us
    ppermute x2, waiting for transfers between devices, extended(): lax.ppermute(head, axis, [((i + 1) % count, i) for i in range(ends)])  5.18 us
    psum x1, blocking collectives, axis_by_axis(): inner = lax.psum(value, inner_axis)  4.96 us
  transfers between devices with their start and end apart: 7, of which 6 were waited for; matrix products, arithmetic and copies ran while one was open for 10% of the time, Pallas kernels for 0%

profile of v1, /device:TPU:0, one launch (start us, length us, event | category | flops | bytes accessed | tf_op | source)
XLA Modules:
  0.0 160.8 jit_solution(10050955853520850819)
XLA Ops:
  7.5 5.0 %collective-permute-start = (bf16[1,24,512]{2,1,0:T(8,128)(2,1)S(1)}, bf16[1,24,512]{2,1,0:T(8,128)(2,1)S(1)}, u32[]{:S(2)}, u32[]{:S(2)}) collective-permute-start(bf16[1,24,512]{2,1,0:T(8,128)(2,1)S(1)} %get-tuple-element.15), channel_id=1, source_target_pairs={{0,4},{4,8},{8,12},{1,5},{5,9},{9,13},{2,6},{6,10},{10,14},{3,7},{... | collective-permute-start | bytes 73736 | tf_op jit(solution)/shard_map/ppermute | solution.py:24
  15.0 3.2 %collective-permute-done.1 = bf16[1,24,512]{2,1,0:T(8,128)(2,1)S(1)} collective-permute-done((bf16[1,24,512]{2,1,0:T(8,128)(2,1)S(1)}, bf16[1,24,512]{2,1,0:T(8,128)(2,1)S(1)}, u32[]{:S(2)}, u32[]{:S(2)}) %collective-permute-start.1) | collective-permute-done | bytes 24608 | tf_op jit(solution)/shard_map/ppermute | solution.py:26
  19.7 4.0 %collective-permute-start.2 = (bf16[18,1,512]{2,1,0:T(2,128)(2,1)}, bf16[18,1,512]{2,1,0:T(2,128)(2,1)}, u32[]{:S(2)}, u32[]{:S(2)}) collective-permute-start(bf16[18,1,512]{2,1,0:T(2,128)(2,1)} %get-tuple-element.12), channel_id=1, source_target_pairs={{0,2},{1,3},{4,6},{5,7},{8,10},{9,11},{12,14},{13,15},{16,18},{17,... | collective-permute-start | bytes 55304 | tf_op jit(solution)/shard_map/ppermute | solution.py:24
  25.0 1.5 fusion.35
  27.8 2.0 %collective-permute-done.3 = bf16[18,1,512]{2,1,0:T(2,128)(2,1)} collective-permute-done((bf16[18,1,512]{2,1,0:T(2,128)(2,1)}, bf16[18,1,512]{2,1,0:T(2,128)(2,1)}, u32[]{:S(2)}, u32[]{:S(2)}) %collective-permute-start.3) | collective-permute-done | bytes 18464 | tf_op jit(solution)/shard_map/ppermute | solution.py:26
  31.2 1.7 %fusion.31 = (f32[16,24]{1,0:T(8,128)S(1)}, f32[16,24]{1,0:T(8,128)S(1)}, f32[16,24,512]{2,1,0:T(8,128)}) fusion(f32[18,26,512]{2,1,0:T(8,128)S(1)} %maximum_convert_fusion, f32[512]{0:T(512)S(1)} %bitcast.83, f32[512]{0:T(512)S(1)} %bitcast.82, f32[512]{0:T(512)S(1)} %bitcast.81, f32[512]{0:T(512)S(1)} %bitcast.80, f32[512]{0:T(512)S(1)} %bitcast.79, ...), kind=kLoop, calls=%fused_computation.65 | loop fusion | flops 4324608 | bytes 8279040 | tf_op jit(solution)/shard_map/reduce_sum | solution.py:60
  33.1 2.5 %all-reduce = (f32[384]{0:T(512)S(1)}, f32[384]{0:T(512)S(1)}) all-reduce(f32[384]{0:T(512)S(1)} %reduce_sum.52, f32[384]{0:T(512)S(1)} %reduce_sum.50), channel_id=1, replica_groups=mesh['slides'=2,'tile'=4,'col'=2,'mp'=2] {'mp'}, use_global_device_ids=true, to_apply=%region_3.0 | all-reduce | flops 768 | bytes 6144 | tf_op jit(solution)/shard_map/psum | solution.py:60
  36.9 2.4 %all_gather.3 = bf16[384,1024]{1,0:T(8,128)(2,1)S(1)} all-gather(bf16[384,512]{1,0:T(8,128)(2,1)S(1)} %fusion.19), channel_id=1, replica_groups=mesh['slides'=2,'tile'=4,'col'=2,'mp'=2] {'mp'}, dimensions={1}, use_global_device_ids=true | all-gather | bytes 1179648 | tf_op jit(solution)/shard_map/all_gather | solution.py:69
  39.3 1.4 fusion.1
  41.5 1.4 convert_multiply_fusion.1
  44.0 2.3 %copy.12 = f32[1,384,512]{1,2,0:T(8,128)} copy(f32[1,384,512]{2,1,0:T(8,128)} %get-tuple-element.10) | data formatting | bytes 1572864 | tf_op jit(solution)/shard_map/mul | solution.py:75
  47.6 5.8 %convert_reduce_fusion = (f32[8,256]{1,0:T(8,128)S(1)}, bf16[384,8,256]{2,0,1:T(8,128)(2,1)}) fusion(bf16[384]{0:T(512)(128)(2,1)S(1)} %copy-done.15, f32[384,8]{0,1:T(8,128)S(1)} %broadcast_multiply_fusion.1, f32[384,8,64]{0,2,1:T(8,128)} %bitcast.71, f32[256,64]{0,1:T(8,128)} %param.12), kind=kOutput, calls=%fused_computation | convolution fusion | flops 608696320 | bytes 2446080 | tf_op jit(solution)/shard_map/the,me->thm/dot_general | solution.py:34
  53.3 5.0 %psum.46 = f32[8,256]{1,0:T(8,128)S(1)} all-reduce(f32[8,256]{1,0:T(8,128)S(1)} %get-tuple-element.29), channel_id=1, replica_groups=mesh['slides'=2,'tile'=4,'col'=2,'mp'=2] {'col'}, use_global_device_ids=true, to_apply=%region_9.0 | all-reduce | flops 2048 | bytes 16384 | tf_op jit(solution)/shard_map/psum | solution.py:12
  58.3 10.3 %psum.47 = f32[8,256]{1,0:T(8,128)S(1)} all-reduce(f32[8,256]{1,0:T(8,128)S(1)} %psum.46), channel_id=1, replica_groups=mesh['slides'=2,'tile'=4,'col'=2,'mp'=2] {'tile'}, use_global_device_ids=true, to_apply=%region_10.0 | all-reduce | flops 2048 | bytes 16384 | tf_op jit(solution)/shard_map/psum | solution.py:13
  68.5 2.6 %fusion.36 = f32[8,64,256]{2,1,0:T(8,128)} fusion(bf16[384,8,64]{0,2,1:T(8,128)(2,1)S(1)} %bitcast.74, bf16[384,8,256]{2,0,1:T(8,128)(2,1)} %get-tuple-element.30), kind=kOutput, calls=%fused_computation.69 | convolution fusion | flops 100663296 | bytes 2490368 | tf_op jit(solution)/shard_map/the,thm->hem/dot_general | solution.py:79
  71.2 2.3 %copy.13 = f32[1,384,512]{1,2,0:T(8,128)} copy(f32[1,384,512]{2,1,0:T(8,128)} %get-tuple-element.11) | data formatting | bytes 1572864 | tf_op jit(solution)/shard_map/mul | solution.py:82
  74.8 5.5 %multiply_convert_fusion = bf16[384,8,256]{2,0,1:T(8,128)(2,1)} fusion(f32[384,8,64]{0,2,1:T(8,128)} %bitcast.73, f32[384,8]{0,1:T(8,128)S(1)} %broadcast_multiply_fusion, f32[256,64]{0,1:T(8,128)S(1)} %copy-done.17), kind=kOutput, calls=%fused_computation.1 | convolution fusion | flops 606339072 | bytes 2437120 | tf_op jit(solution)/shard_map/the,me->thm/dot_general | solution.py:34
  80.3 17.7 %all-reduce.4.cloned.1.call-done = f32[8,64,256]{2,1,0:T(8,128)} async-done(((f32[8,64,256]{2,1,0:T(8,128)}), f32[8,64,256]{2,1,0:T(8,128)}) %all-reduce.4.cloned.1.call-update) | async-done | bytes 524304 | tf_op jit(solution)/shard_map/psum | solution.py:12
  98.0 2.0 %fusion.26 = f32[8,1,384]{2,1,0:T(1,128)S(1)} fusion(bf16[384,8,256]{2,0,1:T(8,128)(2,1)} %multiply_convert_fusion, bf16[8,256,1]{1,0,2:T(8,128)(2,1)S(1)} %get-tuple-element.26), kind=kOutput, calls=%fused_computation.54 | convolution fusion | flops 1572864 | bytes 1589248 | tf_op jit(solution)/shard_map/thm,hm->th/dot_general | solution.py:91
  100.6 38.2 %all-reduce.6.cloned.1.call-done = f32[8,64,256]{2,1,0:T(8,128)} async-done(((f32[8,64,256]{2,1,0:T(8,128)}), f32[8,64,256]{2,1,0:T(8,128)}) %all-reduce.6.cloned.1.call-update) | async-done | bytes 524304 | tf_op jit(solution)/shard_map/psum | solution.py:13
  138.8 2.3 %fusion.21 = f32[8,64,384]{2,1,0:T(8,128)S(1)} fusion(bf16[384,8,256]{2,0,1:T(8,128)(2,1)} %multiply_convert_fusion, f32[8,64,256]{2,1,0:T(8,128)} %all-reduce.6.cloned.1.call-done), kind=kOutput, calls=%fused_computation.45 | convolution fusion | flops 100794368 | bytes 2883584 | tf_op jit(solution)/shard_map/thm,hem->the/dot_general | solution.py:86
  142.3 1.5 fusion.2
  143.8 8.4 %reduce-scatter.2.cloned.1.call-done = bf16[512,384]{0,1:T(8,128)(2,1)} async-done(((bf16[1024,384]{0,1:T(8,128)(2,1)}), bf16[512,384]{0,1:T(8,128)(2,1)}) %reduce-scatter.2.cloned.1.call-update) | async-done | bytes 393232 | tf_op jit(solution)/shard_map/reduce_scatter | solution.py:96
  152.2 2.1 %fusion.15 = bf16[384,512]{1,0:T(8,128)(2,1)} fusion(f32[16,24,512]{2,1,0:T(8,128)} %get-tuple-element.9, bf16[512,384]{0,1:T(8,128)(2,1)} %reduce-scatter.2.cloned.1.call-done), kind=kLoop, calls=%fused_computation.31 | loop fusion | flops 589824 | bytes 1572864 | tf_op jit(solution)/shard_map/convert_element_type | solution.py:107
  (68 shorter events, 16.6 us)
Async XLA Ops:
  6.5 32.7 %copy-start = (bf16[3,1024,512]{2,1,0:T(8,128)(2,1)S(1)}, bf16[3,1024,512]{2,1,0:T(8,128)(2,1)}, u32[]{:S(2)}) copy-start(bf16[3,1024,512]{2,1,0:T(8,128)(2,1)} %param.11) | copy-start | bytes 9437188
  6.5 24.6 %copy-start.3 = (bf16[16,24,512]{2,1,0:T(8,128)(2,1)S(1)}, bf16[16,24,512]{2,1,0:T(8,128)(2,1)}, u32[]{:S(2)}) copy-start(bf16[16,24,512]{2,1,0:T(8,128)(2,1)} %param.7) | copy-start | bytes 1179652
  6.5 91.4 %all-reduce.4.cloned.1.call-start = ((), (), s32[]{:S(2)}) async-start(), calls=%async_computation.1 | async-start | bytes 1048576 | tf_op jit(solution)/shard_map/psum | solution.py:12
  7.5 6.6 %collective-permute-start = (bf16[1,24,512]{2,1,0:T(8,128)(2,1)S(1)}, bf16[1,24,512]{2,1,0:T(8,128)(2,1)S(1)}, u32[]{:S(2)}, u32[]{:S(2)}) collective-permute-start(bf16[1,24,512]{2,1,0:T(8,128)(2,1)S(1)} %get-tuple-element.15), channel_id=1, source_target_pairs={{0,4},{4,8},{8,12},{1,5},{5,9},{9,13},{2,6},{6,10},{10,14},{3,7},{... | collective-permute-start | bytes 73736 | tf_op jit(solution)/shard_map/ppermute | solution.py:24
  12.5 5.7 %collective-permute-start.1 = (bf16[1,24,512]{2,1,0:T(8,128)(2,1)S(1)}, bf16[1,24,512]{2,1,0:T(8,128)(2,1)S(1)}, u32[]{:S(2)}, u32[]{:S(2)}) collective-permute-start(bf16[1,24,512]{2,1,0:T(8,128)(2,1)S(1)} %get-tuple-element.14), channel_id=1, source_target_pairs={{4,0},{8,4},{12,8},{5,1},{9,5},{13,9},{6,2},{10,6},{14,10},{7,3},{... | collective-permute-start | bytes 73736 | tf_op jit(solution)/shard_map/ppermute | solution.py:26
  19.7 8.2 %collective-permute-start.2 = (bf16[18,1,512]{2,1,0:T(2,128)(2,1)}, bf16[18,1,512]{2,1,0:T(2,128)(2,1)}, u32[]{:S(2)}, u32[]{:S(2)}) collective-permute-start(bf16[18,1,512]{2,1,0:T(2,128)(2,1)} %get-tuple-element.12), channel_id=1, source_target_pairs={{0,2},{1,3},{4,6},{5,7},{8,10},{9,11},{12,14},{13,15},{16,18},{17,... | collective-permute-start | bytes 55304 | tf_op jit(solution)/shard_map/ppermute | solution.py:24
  23.7 6.2 %collective-permute-start.3 = (bf16[18,1,512]{2,1,0:T(2,128)(2,1)}, bf16[18,1,512]{2,1,0:T(2,128)(2,1)}, u32[]{:S(2)}, u32[]{:S(2)}) collective-permute-start(bf16[18,1,512]{2,1,0:T(2,128)(2,1)} %get-tuple-element.13), channel_id=1, source_target_pairs={{2,0},{3,1},{6,4},{7,5},{10,8},{11,9},{14,12},{15,13},{18,16},{19,... | collective-permute-start | bytes 55304 | tf_op jit(solution)/shard_map/ppermute | solution.py:26
  27.8 3.3 %copy-start.6 = (f32[1,1,512]{2,1,0:T(1,128)S(1)}, f32[1,1,512]{2,1,0:T(1,128)}, u32[]{:S(2)}) copy-start(f32[1,1,512]{2,1,0:T(1,128)} %get-tuple-element.16) | copy-start | bytes 6148
  27.8 3.3 %copy-start.7 = (f32[1,1,512]{2,1,0:T(1,128)S(1)}, f32[1,1,512]{2,1,0:T(1,128)}, u32[]{:S(2)}) copy-start(f32[1,1,512]{2,1,0:T(1,128)} %get-tuple-element.17) | copy-start | bytes 6148
  27.8 3.3 %copy-start.8 = (f32[1,1,512]{2,1,0:T(1,128)S(1)}, f32[1,1,512]{2,1,0:T(1,128)}, u32[]{:S(2)}) copy-start(f32[1,1,512]{2,1,0:T(1,128)} %get-tuple-element.18) | copy-start | bytes 6148
  27.8 3.4 %copy-start.9 = (f32[1,1,512]{2,1,0:T(1,128)S(1)}, f32[1,1,512]{2,1,0:T(1,128)}, u32[]{:S(2)}) copy-start(f32[1,1,512]{2,1,0:T(1,128)} %get-tuple-element.19) | copy-start | bytes 6148
  27.8 3.4 %copy-start.10 = (f32[1,1,512]{2,1,0:T(1,128)S(1)}, f32[1,1,512]{2,1,0:T(1,128)}, u32[]{:S(2)}) copy-start(f32[1,1,512]{2,1,0:T(1,128)} %get-tuple-element.20) | copy-start | bytes 6148
  27.8 3.4 %copy-start.11 = (f32[1,1,512]{2,1,0:T(1,128)S(1)}, f32[1,1,512]{2,1,0:T(1,128)}, u32[]{:S(2)}) copy-start(f32[1,1,512]{2,1,0:T(1,128)} %get-tuple-element.21) | copy-start | bytes 6148
  27.8 3.4 %copy-start.12 = (f32[1,1,512]{2,1,0:T(1,128)S(1)}, f32[1,1,512]{2,1,0:T(1,128)}, u32[]{:S(2)}) copy-start(f32[1,1,512]{2,1,0:T(1,128)} %get-tuple-element.22) | copy-start | bytes 6148
  27.8 3.4 %copy-start.13 = (f32[1,1,512]{2,1,0:T(1,128)S(1)}, f32[1,1,512]{2,1,0:T(1,128)}, u32[]{:S(2)}) copy-start(f32[1,1,512]{2,1,0:T(1,128)} %get-tuple-element.23) | copy-start | bytes 6148
  27.8 3.4 %copy-start.14 = (f32[1,1,512]{2,1,0:T(1,128)S(1)}, f32[1,1,512]{2,1,0:T(1,128)}, u32[]{:S(2)}) copy-start(f32[1,1,512]{2,1,0:T(1,128)} %get-tuple-element.24) | copy-start | bytes 6148
  42.8 4.7 %copy-start.15 = (bf16[384]{0:T(512)(128)(2,1)S(1)}, bf16[384]{0:T(512)(128)(2,1)}, u32[]{:S(2)}) copy-start(bf16[384]{0:T(512)(128)(2,1)} %convert_element_type.95) | copy-start | bytes 2308
  71.2 3.6 %copy-start.17 = (f32[256,64]{0,1:T(8,128)S(1)}, f32[256,64]{0,1:T(8,128)}, u32[]{:S(2)}) copy-start(f32[256,64]{0,1:T(8,128)} %param.12) | copy-start | bytes 196612
  71.2 67.6 %all-reduce.6.cloned.1.call-start = ((), (), s32[]{:S(2)}) async-start(), calls=%async_computation.2 | async-start | bytes 1048576 | tf_op jit(solution)/shard_map/psum | solution.py:13
  98.0 54.2 %reduce-scatter.2.cloned.1.call-start = ((), (), s32[]{:S(2)}) async-start(), calls=%async_computation.3 | async-start | bytes 1179648 | tf_op jit(solution)/shard_map/reduce_scatter | solution.py:96
  98.0 2.0 %copy-start.1 = (bf16[384,8,256]{2,0,1:T(8,128)(2,1)S(1)}, bf16[384,8,256]{2,0,1:T(8,128)(2,1)}, u32[]{:S(2)}) copy-start(bf16[384,8,256]{2,0,1:T(8,128)(2,1)} %multiply_convert_fusion) | copy-start | bytes 4718596
  138.8 2.3 %copy-start.2 = (bf16[384,8,256]{2,0,1:T(8,128)(2,1)S(1)}, bf16[384,8,256]{2,0,1:T(8,128)(2,1)}, u32[]{:S(2)}) copy-start(bf16[384,8,256]{2,0,1:T(8,128)(2,1)} %multiply_convert_fusion) | copy-start | bytes 4718596
  138.8 2.3 %copy-start.5 = (f32[8,64,256]{2,1,0:T(8,128)S(1)}, f32[8,64,256]{2,1,0:T(8,128)}, u32[]{:S(2)}) copy-start(f32[8,64,256]{2,1,0:T(8,128)} %all-reduce.6.cloned.1.call-done) | copy-start | bytes 1572868
  141.1 1.2 copy-start.16
  (1 other events, 0.8 us)
Sparse Core Ops, SparseCore 0:
  71.3 26.5 all-reduce.3
  100.4 38.2 all-reduce.5
  143.9 8.2 reduce-scatter.1
